TPU v7x, 32 devices: a whole 2x2x4 slice. The times are simulated.
32 devices in a mesh: grp: 2 (over x), gx: 16 (over z, y, core).
Axes of the slice: x: 2, y: 2, z: 4, core: 2. Of those that a mesh axis runs over, the one named last changes fastest.
Arguments:
- pressure_source: float32 [128, 128, 128], P(('grp', 'gx')), parts along dimension 0
- permeability: float32 [128, 128, 128], P(('grp', 'gx')), parts along dimension 0, may hold values from 0.1 to 10
- basis: float32 [40, 128, 128, 128], P(None, ('grp', 'gx')), parts along dimension 1, may hold values from -0.084 to 0.084
- widths: int32 [32], P(('grp', 'gx')), parts along dimension 0, may hold values from 8 to 40, as said below
- extents: int32 [32], P(('grp', 'gx')), parts along dimension 0, may hold values from 1 to 2, as said below
- coarse_owner: int32 [32], P('grp'), parts along dimension 0, may hold values from 0 to 15, as said below
- coarse_inverse: float32 [1280, 640], P(('grp', 'gx')), parts along dimension 0, as said below
Outputs:
- pressure: float32 [128, 128, 128], P(('grp', 'gx')), parts along dimension 0
- residual: float32 [128, 128, 128], P(('grp', 'gx')), parts along dimension 0
There are 2 independent parts, one for each index of `grp`. A program takes and returns all parts, laid end to end along the dimension named above; each array names one. Nothing has to cross between parts.
Inputs may be any that keep to these rules, and one draw needn't show every extreme that they name: `widths`: every draw has a subdomain with 40 vectors and one with 8. `extents`: every draw has a subdomain with 2 margin planes and one with 1. `coarse_owner`: A permutation of the subdomains. `coarse_inverse`: block row b holds the coarse rows of subdomain coarse_owner[b]; the matrix of those rows in subdomain order is symmetric positive definite.
All inputs are finite; a program needn't handle non-finite values.
Results may differ from a plain program's by a relative error of at most 0.0003.
Values sent between devices are 32-bit elements; how exact they have to be, the bound alone decides.
A program may use at most 128 MiB of HBM per device.

v0:
```python
import jax
import jax.numpy as jnp
from jax import lax
from jax.sharding import PartitionSpec as P

OV = 2
SWEEPS = 6
ITERS = 2


OMEGA = 0.8
highest = lax.Precision.HIGHEST


def with_halo(block, sides, width):
    for axis, dim in sides:
        count = lax.axis_size(axis)
        forward = [(i, i + 1) for i in range(count - 1)]
        backward = [(target, source) for source, target in forward]
        low = lax.ppermute(
            lax.slice_in_dim(block, block.shape[dim] - width, None, axis=dim), axis, forward
        )
        high = lax.ppermute(lax.slice_in_dim(block, 0, width, axis=dim), axis, backward)
        block = jnp.concatenate([low, block, high], axis=dim)
    return block


def harmonic(left, right):
    return 2.0 * left * right / (left + right)


def coefficients(padded):
    centre = padded[1:-1, 1:-1, 1:-1]
    lower_x = harmonic(centre, padded[:-2, 1:-1, 1:-1])
    upper_x = harmonic(centre, padded[2:, 1:-1, 1:-1])
    lower_y = harmonic(centre, padded[1:-1, :-2, 1:-1])
    upper_y = harmonic(centre, padded[1:-1, 2:, 1:-1])
    lower_z = harmonic(centre, padded[1:-1, 1:-1, :-2])
    upper_z = harmonic(centre, padded[1:-1, 1:-1, 2:])
    diagonal = lower_x + upper_x + lower_y + upper_y + lower_z + upper_z
    return (lower_x, upper_x, lower_y, upper_y, lower_z, upper_z, diagonal)


def stencil(padded, couplings):
    centre = padded[1:-1, 1:-1, 1:-1]
    beside = couplings[0] * padded[:-2, 1:-1, 1:-1] + couplings[1] * padded[2:, 1:-1, 1:-1]
    beside = beside + couplings[2] * padded[1:-1, :-2, 1:-1] + couplings[3] * padded[1:-1, 2:, 1:-1]
    beside = beside + couplings[4] * padded[1:-1, 1:-1, :-2] + couplings[5] * padded[1:-1, 1:-1, 2:]
    return couplings[6] * centre - beside


def smoother(rhs_values, couplings, inside):
    rhs_values = jnp.where(inside, rhs_values, 0.0)
    update = jnp.zeros_like(rhs_values)
    for sweep in range(SWEEPS):
        action = stencil(jnp.pad(update, 1), couplings)
        update = jnp.where(inside, update + OMEGA * (rhs_values - action) / couplings[6], 0.0)
    return update


def pad_sides(values_in):
    return jnp.pad(values_in, ((0, 0), (1, 1), (1, 1)))


def per_device(pressure_source, permeability, basis, widths, extents, coarse_owner, coarse_inverse):
    own_planes = pressure_source.shape[0]
    devices_x = lax.axis_size("gx")
    device_index = lax.axis_index("gx")
    first_plane = device_index * own_planes
    grid_planes = own_planes * devices_x
    planes = own_planes + 2 * OV
    haloed = with_halo(permeability, (("gx", 0),), OV + 1)
    halo_plane = first_plane - (OV + 1) + jnp.arange(planes + 2, dtype=jnp.int32)
    haloed = jnp.where((halo_plane < 0)[:, None, None], permeability[0][None], haloed)
    haloed = jnp.where((halo_plane >= grid_planes)[:, None, None], permeability[-1][None], haloed)
    wide_couplings = coefficients(jnp.pad(haloed, ((0, 0), (1, 1), (1, 1)), mode="edge"))
    own_couplings = tuple((component[OV : OV + own_planes] for component in wide_couplings))
    wide_plane = first_plane - OV + jnp.arange(planes, dtype=jnp.int32)
    extent = extents[0]
    inside = (wide_plane >= first_plane - extent) & (wide_plane < first_plane + own_planes + extent)
    inside = (inside & (wide_plane >= 0) & (wide_plane < grid_planes))[:, None, None]
    column_mask = (jnp.arange(basis.shape[0], dtype=jnp.int32) < widths[0]).astype(jnp.float32)
    selector = (coarse_owner == device_index).astype(jnp.float32)
    basis_rows = basis.reshape(basis.shape[0], -1)

    def extend(values_in):
        return with_halo(values_in, (("gx", 0),), OV)

    def add_columns(projection_piece):
        return jnp.dot(coarse_inverse, projection_piece, precision=highest)

    def precondition(wide_residual):
        update = smoother(wide_residual, wide_couplings, inside)
        spilled = jnp.concatenate([update[:OV], update[OV + own_planes :]], axis=0)
        returned = with_halo(spilled, (("gx", 0),), OV)
        local_part = update[OV : OV + own_planes]
        local_part = local_part.at[:OV].add(returned[:OV])
        local_part = local_part.at[own_planes - OV :].add(returned[3 * OV :])
        residual_own = wide_residual[OV : OV + own_planes]
        projected = jnp.dot(basis_rows, residual_own.reshape(-1), precision=highest) * column_mask
        solved = add_columns(lax.all_gather(projected, "gx", axis=0, tiled=True))
        everyone = lax.all_gather(solved[None, :], "gx", axis=0, tiled=True)
        coarse = jnp.dot(selector, everyone, precision=highest) * column_mask
        correction = jnp.dot(coarse, basis_rows, precision=highest).reshape(residual_own.shape)
        return local_part + correction

    def residual_product(left, right):
        return lax.psum(jnp.sum(left * right), "gx")

    pressure = jnp.zeros_like(pressure_source)
    residual = pressure_source
    wide_residual = extend(residual)
    preconditioned = precondition(wide_residual)
    direction = preconditioned
    product_now = residual_product(residual, preconditioned)
    for iteration in range(ITERS):
        padded = with_halo(direction, (("gx", 0),), 1)
        image = stencil(pad_sides(padded), own_couplings)
        step_length = product_now / lax.psum(jnp.sum(direction * image), "gx")
        pressure = pressure + step_length * direction
        residual = residual - step_length * image
        if iteration + 1 < ITERS:
            wide_residual = extend(residual)
            preconditioned = precondition(wide_residual)
            product_next = residual_product(residual, preconditioned)
            direction = preconditioned + product_next / product_now * direction
            product_now = product_next
    return (pressure, residual)


def solution(mesh):
    placed = (
        P(("grp", "gx"), None, None),
        P(("grp", "gx"), None, None),
        P(None, ("grp", "gx"), None, None),
        P(("grp", "gx")),
        P(("grp", "gx")),
        P("grp"),
        P(("grp", "gx"), None),
    )
    return jax.shard_map(
        per_device,
        mesh=mesh,
        in_specs=placed,
        out_specs=(P(("grp", "gx"), None, None), P(("grp", "gx"), None, None)),
        check_vma=False,
    )
```

profile of v0, /device:TPU:0, one launch (start us, length us, event | category | flops | bytes accessed | tf_op | source)
XLA Modules:
  0.0 379.6 jit_solution(11138508649424882973)
XLA Ops:
  0.6 1.1 fusion.248
  1.7 2.4 collective-permute-start.2
  4.1 1.3 collective-permute-start.3
  5.4 1.7 fusion.247
  7.1 5.8 %collective-permute-start = (f32[2,128,128]{2,1,0:T(8,128)}, f32[2,128,128]{2,1,0:T(8,128)}, u32[]{:S(2)}, u32[]{:S(2)}) collective-permute-start(f32[2,128,128]{2,1,0:T(8,128)} %get-tuple-element.96), channel_id=1, source_target_pairs={{0,1},{1,2},{2,3},{3,4},{4,5},{5,6},{6,7},{7,8},{8,9},{9,10},{10,1... | collective-permute-start | bytes 393224 | tf_op jit(solution)/shard_map/ppermute | solution.py:20
  12.9 1.3 collective-permute-start.1
  15.5 1.3 dynamic-slice.32
  17.4 16.9 %fusion.21 = f32[40]{0:T(128)S(1)} fusion(f32[4,128,128,1]{2,3,1,0:T(1,128)} %bitcast.96, f32[40,4,128,128]{3,2,1,0:T(8,128)} %param.17, s32[]{:T(128)} %bitcast.82), kind=kOutput, calls=%fused_computation.90 | convolution fusion | flops 31457360 | bytes 10748068 | tf_op jit(solution)/shard_map/dot_general | solution.py:100
  34.4 0.2 dynamic-update-slice.12
  34.6 34.9 %all-reduce.13 = f32[640]{0:T(1024)S(1)} all-reduce(f32[640]{0:T(1024)S(1)} %dynamic-update-slice.12), channel_id=1, replica_groups=mesh['grp'=2,'gx'=16] {'gx'}, use_global_device_ids=true, to_apply=%add.13 | all-reduce | flops 640 | bytes 5120
  69.5 0.2 convolution_bitcast_fusion.3
  69.6 0.2 dynamic-update-slice.13
  69.9 29.6 %all-reduce.14 = f32[640]{0:T(1024)S(1)} all-reduce(f32[640]{0:T(1024)S(1)} %dynamic-update-slice.13), channel_id=2, replica_groups=mesh['grp'=2,'gx'=16] {'gx'}, use_global_device_ids=true, to_apply=%add.14 | all-reduce | flops 640 | bytes 5120
  99.6 9.9 %copy.38 = f32[5,8,512,128]{3,1,2,0:T(8,128)S(1)} copy(f32[5,8,512,128]{3,2,1,0:T(8,128)} %bitcast.88) | data formatting | bytes 20971520
  109.5 5.9 %copy.20 = f32[5,8,512,128]{3,2,1,0:T(8,128)} copy(f32[5,8,512,128]{3,1,2,0:T(8,128)S(1)} %copy.38) | data formatting | bytes 20971520
  115.9 0.2 fusion.240
  116.1 0.9 add_add_fusion
  117.1 0.9 copy-done.4
  118.0 1.6 divide_select_fusion.1
  119.6 1.7 broadcast_select_fusion.7
  121.2 1.8 broadcast_select_fusion.6
  123.1 2.2 broadcast_select_fusion.5
  125.3 1.8 broadcast_select_fusion.4
  127.2 1.7 fusion.201
  128.9 1.8 collective-permute-start.4
  130.7 11.1 %fusion.2 = f32[1,4,128,128]{3,0,2,1:T(1,128)S(1)} fusion(f32[40,1,1,1]{0,1,3,2:T(1,128)S(1)} %fusion.15, f32[4,128,128,40]{2,1,0,3:T(8,128)S(1)} %bitcast.91), kind=kOutput, calls=%fused_computation.3 | convolution fusion | flops 31457280 | bytes 10748064 | tf_op jit(solution)/shard_map/dot_general | solution.py:104
  141.8 1.3 collective-permute-start.5
  143.2 1.9 collective-permute-done.5
  145.2 5.0 %collective-permute-start.6 = (f32[1,128,128]{2,1,0:T(8,128)S(1)}, f32[1,128,128]{2,1,0:T(8,128)S(1)}, u32[]{:S(2)}, u32[]{:S(2)}) collective-permute-start(f32[1,128,128]{2,1,0:T(8,128)S(1)} %get-tuple-element.94), channel_id=1, source_target_pairs={{0,1},{1,2},{2,3},{3,4},{4,5},{5,6},{6,7},{7,8},{8,9},{9,10},{10,1... | collective-permute-start | bytes 196616 | tf_op jit(solution)/shard_map/ppermute | solution.py:20
  150.2 1.5 collective-permute-start.7
  151.6 1.7 collective-permute-done.7
  153.3 0.3 select_maximum_fusion.2
  153.6 1.7 multiply_reduce_fusion.2
  155.3 32.6 %all-reduce.17 = (f32[]{:T(128)}, f32[]{:T(128)}) all-reduce(f32[]{:T(128)} %get-tuple-element.51, f32[]{:T(128)} %get-tuple-element.50), channel_id=1, replica_groups=mesh['grp'=2,'gx'=16] {'gx'}, use_global_device_ids=true, to_apply=%region_1.2 | all-reduce | flops 2 | bytes 16 | tf_op jit(solution)/shard_map/psum | solution.py:108
  189.1 1.1 multiply_subtract_fusion.1
  190.2 0.7 fusion.245
  190.9 16.6 %fusion.18 = f32[40]{0:T(128)S(1)} fusion(f32[4,128,128,1]{2,3,1,0:T(1,128)S(1)} %bitcast.95, f32[40,4,128,128]{3,2,1,0:T(8,128)} %param.17, s32[]{:T(128)} %bitcast.84), kind=kOutput, calls=%fused_computation.89 | convolution fusion | flops 31457360 | bytes 10748068 | tf_op jit(solution)/shard_map/dot_general | solution.py:100
  207.5 0.2 dynamic-update-slice.14
  207.7 29.5 %all-reduce.15 = f32[640]{0:T(1024)S(1)} all-reduce(f32[640]{0:T(1024)S(1)} %dynamic-update-slice.14), channel_id=1, replica_groups=mesh['grp'=2,'gx'=16] {'gx'}, use_global_device_ids=true, to_apply=%add.15 | all-reduce | flops 640 | bytes 5120
  237.2 2.4 collective-permute-start.8
  239.6 1.3 collective-permute-start.9
  241.1 0.2 dynamic-update-slice.15
  241.3 30.6 %all-reduce.16 = f32[640]{0:T(1024)S(1)} all-reduce(f32[640]{0:T(1024)S(1)} %dynamic-update-slice.15), channel_id=3, replica_groups=mesh['grp'=2,'gx'=16] {'gx'}, use_global_device_ids=true, to_apply=%add.16 | all-reduce | flops 640 | bytes 5120
  272.1 3.3 divide_select_fusion
  275.4 1.6 broadcast_select_fusion.3
  277.1 1.8 broadcast_select_fusion.2
  278.9 1.8 broadcast_select_fusion.1
  280.8 1.8 broadcast_select_fusion
  282.6 1.7 fusion.200
  284.3 1.5 collective-permute-start.10
  285.9 11.1 %fusion = f32[1,4,128,128]{3,0,2,1:T(1,128)S(1)} fusion(f32[40,1,1,1]{0,1,3,2:T(1,128)S(1)} %fusion.17, f32[4,128,128,40]{2,1,0,3:T(8,128)S(1)} %bitcast.94), kind=kOutput, calls=%fused_computation.1 | convolution fusion | flops 31457280 | bytes 10748064 | tf_op jit(solution)/shard_map/dot_general | solution.py:104
  297.0 1.3 collective-permute-start.11
  298.3 1.9 collective-permute-done.11
  300.3 1.4 multiply_reduce_fusion.1
  301.6 32.6 %psum.30 = f32[]{:T(128)} all-reduce(f32[]{:T(128)} %get-tuple-element.56), channel_id=1, replica_groups=mesh['grp'=2,'gx'=16] {'gx'}, use_global_device_ids=true, to_apply=%region_5.6 | all-reduce | flops 1 | bytes 8 | tf_op jit(solution)/shard_map/psum | solution.py:108
  335.6 1.1 multiply_add_fusion.1
  336.7 1.3 collective-permute-start.12
  338.0 1.3 collective-permute-start.13
  339.3 1.8 collective-permute-done.13
  341.1 0.3 select_maximum_fusion
  341.4 2.6 multiply_reduce_fusion
  344.0 30.6 %psum.31 = f32[]{:T(128)} all-reduce(f32[]{:T(128)} %get-tuple-element.54), channel_id=1, replica_groups=mesh['grp'=2,'gx'=16] {'gx'}, use_global_device_ids=true, to_apply=%region_7.8 | all-reduce | flops 1 | bytes 8 | tf_op jit(solution)/shard_map/psum | solution.py:119
  375.9 1.8 multiply_add_fusion
  377.7 1.7 multiply_subtract_fusion
  (68 shorter events, 1.2 us)
Async XLA Ops:
  0.6 68.8 %copy-start = (f32[40,640]{1,0:T(8,128)S(1)}, f32[40,640]{1,0:T(8,128)}, u32[]{:S(2)}) copy-start(f32[40,640]{1,0:T(8,128)} %param.21) | copy-start | bytes 307204
  1.7 113.9 %collective-permute-start.2 = (f32[3,128,128]{2,1,0:T(8,128)S(1)}, f32[3,128,128]{2,1,0:T(8,128)S(1)}, u32[]{:S(2)}, u32[]{:S(2)}) collective-permute-start(f32[3,128,128]{2,1,0:T(8,128)S(1)} %get-tuple-element.100), channel_id=1, source_target_pairs={{0,1},{1,2},{2,3},{3,4},{4,5},{5,6},{6,7},{7,8},{8,9},{9,10},{10,1... | collective-permute-start | bytes 589832 | tf_op jit(solution)/shard_map/ppermute | solution.py:20
  4.1 111.5 %collective-permute-start.3 = (f32[3,128,128]{2,1,0:T(8,128)S(1)}, f32[3,128,128]{2,1,0:T(8,128)S(1)}, u32[]{:S(2)}, u32[]{:S(2)}) collective-permute-start(f32[3,128,128]{2,1,0:T(8,128)S(1)} %get-tuple-element.101), channel_id=1, source_target_pairs={{1,0},{2,1},{3,2},{4,3},{5,4},{6,5},{7,6},{8,7},{9,8},{10,9},{11,1... | collective-permute-start | bytes 589832 | tf_op jit(solution)/shard_map/ppermute | solution.py:23
  7.1 109.9 %collective-permute-start = (f32[2,128,128]{2,1,0:T(8,128)}, f32[2,128,128]{2,1,0:T(8,128)}, u32[]{:S(2)}, u32[]{:S(2)}) collective-permute-start(f32[2,128,128]{2,1,0:T(8,128)} %get-tuple-element.96), channel_id=1, source_target_pairs={{0,1},{1,2},{2,3},{3,4},{4,5},{5,6},{6,7},{7,8},{8,9},{9,10},{10,1... | collective-permute-start | bytes 393224 | tf_op jit(solution)/shard_map/ppermute | solution.py:20
  12.9 104.1 %collective-permute-start.1 = (f32[2,128,128]{2,1,0:T(8,128)}, f32[2,128,128]{2,1,0:T(8,128)}, u32[]{:S(2)}, u32[]{:S(2)}) collective-permute-start(f32[2,128,128]{2,1,0:T(8,128)} %get-tuple-element.97), channel_id=1, source_target_pairs={{1,0},{2,1},{3,2},{4,3},{5,4},{6,5},{7,6},{8,7},{9,8},{10,9},{11,1... | collective-permute-start | bytes 393224 | tf_op jit(solution)/shard_map/ppermute | solution.py:23
  109.5 6.0 %copy-start.7 = (s32[16]{0:T(128)S(1)}, s32[16]{0:T(128)}, u32[]{:S(2)}) copy-start(s32[16]{0:T(128)} %param.20) | copy-start | bytes 196
  109.5 6.1 %copy-start.5 = (f32[4,128,128]{2,1,0:T(8,128)S(1)}, f32[4,128,128]{2,1,0:T(8,128)}, u32[]{:S(2)}) copy-start(f32[4,128,128]{2,1,0:T(8,128)} %param.16) | copy-start | bytes 786436
  115.4 2.5 copy-start.1
  117.0 36.6 %copy-start.6 = (f32[8,128,128]{2,1,0:T(8,128)}, f32[8,128,128]{2,1,0:T(8,128)S(1)}, u32[]{:S(2)}) copy-start(f32[8,128,128]{2,1,0:T(8,128)S(1)} %get-tuple-element.67) | copy-start | bytes 1572868
  117.1 0.9 copy-start.4
  121.2 9.5 %slice-start = ((s8[10485760]{0:T(1024)(128)(4,1)}), s8[4194304]{0:T(1024)(128)(4,1)S(1)}, s32[]{:S(2)}) async-start(s8[10485760]{0:T(1024)(128)(4,1)} %bitcast.89), calls=%async_computation | async-start | bytes 8388608
  123.1 7.6 %slice-start.1 = ((s8[10485760]{0:T(1024)(128)(4,1)}), s8[4194304]{0:T(1024)(128)(4,1)S(1)}, s32[]{:S(2)}) async-start(s8[10485760]{0:T(1024)(128)(4,1)} %bitcast.89), calls=%async_computation.1 | async-start | bytes 8388608
  125.3 5.4 %slice-start.2 = ((s8[10485760]{0:T(1024)(128)(4,1)}), s8[2097152]{0:T(1024)(128)(4,1)S(1)}, s32[]{:S(2)}) async-start(s8[10485760]{0:T(1024)(128)(4,1)} %bitcast.89), calls=%async_computation.2 | async-start | bytes 4194304
  128.9 14.2 %collective-permute-start.4 = (f32[2,128,128]{2,1,0:T(8,128)S(1)}, f32[2,128,128]{2,1,0:T(8,128)S(1)}, u32[]{:S(2)}, u32[]{:S(2)}) collective-permute-start(f32[2,128,128]{2,1,0:T(8,128)S(1)} %get-tuple-element.89), channel_id=1, source_target_pairs={{0,1},{1,2},{2,3},{3,4},{4,5},{5,6},{6,7},{7,8},{8,9},{9,10},{10,1... | collective-permute-start | bytes 393224 | tf_op jit(solution)/shard_map/ppermute | solution.py:20
  141.8 3.2 collective-permute-start.5
  145.2 10.2 %copy-start.2 = (f32[4,128,128]{2,1,0:T(8,128)}, f32[4,128,128]{2,1,0:T(8,128)S(1)}, u32[]{:S(2)}) copy-start(f32[4,128,128]{2,1,0:T(8,128)S(1)} %add.422) | copy-start | bytes 786436
  145.2 6.4 %collective-permute-start.6 = (f32[1,128,128]{2,1,0:T(8,128)S(1)}, f32[1,128,128]{2,1,0:T(8,128)S(1)}, u32[]{:S(2)}, u32[]{:S(2)}) collective-permute-start(f32[1,128,128]{2,1,0:T(8,128)S(1)} %get-tuple-element.94), channel_id=1, source_target_pairs={{0,1},{1,2},{2,3},{3,4},{4,5},{5,6},{6,7},{7,8},{8,9},{9,10},{10,1... | collective-permute-start | bytes 196616 | tf_op jit(solution)/shard_map/ppermute | solution.py:20
  150.2 3.1 collective-permute-start.7
  237.2 34.9 %collective-permute-start.8 = (f32[2,128,128]{2,1,0:T(8,128)}, f32[2,128,128]{2,1,0:T(8,128)}, u32[]{:S(2)}, u32[]{:S(2)}) collective-permute-start(f32[2,128,128]{2,1,0:T(8,128)} %get-tuple-element.92), channel_id=1, source_target_pairs={{0,1},{1,2},{2,3},{3,4},{4,5},{5,6},{6,7},{7,8},{8,9},{9,10},{10,1... | collective-permute-start | bytes 393224 | tf_op jit(solution)/shard_map/ppermute | solution.py:20
  239.6 32.5 %collective-permute-start.9 = (f32[2,128,128]{2,1,0:T(8,128)}, f32[2,128,128]{2,1,0:T(8,128)}, u32[]{:S(2)}, u32[]{:S(2)}) collective-permute-start(f32[2,128,128]{2,1,0:T(8,128)} %get-tuple-element.93), channel_id=1, source_target_pairs={{1,0},{2,1},{3,2},{4,3},{5,4},{6,5},{7,6},{8,7},{9,8},{10,9},{11,1... | collective-permute-start | bytes 393224 | tf_op jit(solution)/shard_map/ppermute | solution.py:23
  277.0 8.8 %slice-start.3 = ((s8[10485760]{0:T(1024)(128)(4,1)}), s8[4194304]{0:T(1024)(128)(4,1)S(1)}, s32[]{:S(2)}) async-start(s8[10485760]{0:T(1024)(128)(4,1)} %bitcast.92), calls=%async_computation.3 | async-start | bytes 8388608
  278.9 7.0 %slice-start.4 = ((s8[10485760]{0:T(1024)(128)(4,1)}), s8[4194304]{0:T(1024)(128)(4,1)S(1)}, s32[]{:S(2)}) async-start(s8[10485760]{0:T(1024)(128)(4,1)} %bitcast.92), calls=%async_computation.4 | async-start | bytes 8388608
  280.8 5.1 %slice-start.5 = ((s8[10485760]{0:T(1024)(128)(4,1)}), s8[2097152]{0:T(1024)(128)(4,1)S(1)}, s32[]{:S(2)}) async-start(s8[10485760]{0:T(1024)(128)(4,1)} %bitcast.92), calls=%async_computation.5 | async-start | bytes 4194304
  284.3 14.0 %collective-permute-start.10 = (f32[2,128,128]{2,1,0:T(8,128)S(1)}, f32[2,128,128]{2,1,0:T(8,128)S(1)}, u32[]{:S(2)}, u32[]{:S(2)}) collective-permute-start(f32[2,128,128]{2,1,0:T(8,128)S(1)} %get-tuple-element.87), channel_id=1, source_target_pairs={{0,1},{1,2},{2,3},{3,4},{4,5},{5,6},{6,7},{7,8},{8,9},{9,10},{10,1... | collective-permute-start | bytes 393224 | tf_op jit(solution)/shard_map/ppermute | solution.py:20
  297.0 3.2 collective-permute-start.11
  336.6 7.4 %copy-start.3 = (f32[4,128,128]{2,1,0:T(8,128)}, f32[4,128,128]{2,1,0:T(8,128)S(1)}, u32[]{:S(2)}) copy-start(f32[4,128,128]{2,1,0:T(8,128)S(1)} %multiply_add_fusion.1) | copy-start | bytes 786436
  336.7 2.6 collective-permute-start.12
  338.0 3.1 collective-permute-start.13
where the time goes:
time: 387 us; the launch traced here: 380 us
  blocking collectives  220 us (57%)
  matrix products  56.3 us (15%)
  other arithmetic  36.1 us (9%)
  starting transfers between devices  29.3 us (8%)
  local copies, waits for them, and re-layouts  23.1 us (6%)
  waiting for transfers between devices  7.35 us (2%)
  between operations  7.24 us (2%)
    unnamed x4, blocking collectives  125 us
    psum x2, blocking collectives, residual_product(): return lax.psum(jnp.sum(left * right), 'gx')  65.1 us
    dot_general x2, matrix products, precondition(): jnp.dot(basis_rows, residual_own.reshape(-1), precision=highest)  33.5 us
    psum x1, blocking collectives, per_device(): step_length = product_now / lax.psum(jnp.sum(direction * image), 'gx')  30.6 us
    select_n x12, other arithmetic, smoother(): jnp.where(inside, update + OMEGA * (rhs_values - action) / couplings[6],...  23 us
    dot_general x2, matrix products, precondition(): jnp.dot(coarse, basis_rows, precision=highest).reshape(residual_own.shape)  22.2 us
    ppermute x7, starting transfers between devices, with_halo(): lax.ppermute(lax.slice_in_dim(block, block.shape[dim] - width, None, axis...  20.1 us
    unnamed x41, local copies, waits for them, and re-layouts  19 us
  transfers between devices with their start and end apart: 14, of which 4 were waited for; matrix products, arithmetic and copies ran while one was open for 16% of the time, Pallas kernels for 0%

commit v1 on v0

v1 whole, which is shorter than its diff:
```python
import functools

import jax
import jax.numpy as jnp
from jax import lax
from jax.experimental import pallas as pl
from jax.experimental.pallas import tpu as pltpu
from jax.sharding import PartitionSpec as P

OV = 2
SWEEPS = 6
OMEGA = 0.8
PAD = 8
ROWS = 32
HALF = 64
GROUP = 8
HIGHEST = lax.Precision.HIGHEST
MESH = pl.DeviceIdType.MESH
F32 = jnp.float32
PERM, RHS, SPILL0, NEAR0, FAR0, SPILL1, NEAR1 = range(7)


def kernel(
    n, src_ref, perm_ref, width_ref, extent_ref, owner_ref, inverse_ref, basis_ref,
    pressure_ref, residual_ref,
    basis, kx, fx, vx, weights, scale, diagonal, rhs, fields, spills, zx, z1x, image,
    rows, coarse_rows, spread, cast, basis_sem, send_sem, recv_sem, cast_send, cast_recv,
):
    me = lax.axis_index("gx")
    own, ny, nz = src_ref.shape
    wide = own + 2 * OV
    modes = basis_ref.shape[0]
    groups = modes // GROUP

    def basis_copy(g):
        part = pl.ds(g * GROUP, GROUP)
        return pltpu.make_async_copy(basis_ref.at[part], basis.at[part], basis_sem.at[g])

    for g in range(groups):
        basis_copy(g).start()

    barrier = pltpu.get_barrier_semaphore()

    @pl.loop(1, n)
    def _(k):
        pl.semaphore_signal(
            barrier, inc=1, device_id={"gx": lax.rem(me + k, n)}, device_id_type=MESH
        )

    pl.semaphore_wait(barrier, n - 1)

    body = pl.ds(PAD, ny)
    plans = {
        PERM: (
            perm_ref.at[pl.ds(0, OV + 1)], kx.at[pl.ds(own + OV + 1, OV + 1)],
            perm_ref.at[pl.ds(own - OV - 1, OV + 1)], kx.at[pl.ds(0, OV + 1)],
        ),
        RHS: (
            src_ref.at[pl.ds(0, OV)], fx.at[pl.ds(own + OV, OV)],
            src_ref.at[pl.ds(own - OV, OV)], fx.at[pl.ds(0, OV)],
        ),
        NEAR0: (
            zx.at[OV + 1, body], zx.at[own + OV + 1, body],
            zx.at[own + OV, body], zx.at[OV, body],
        ),
        FAR0: (
            zx.at[pl.ds(OV + 2, OV), body], zx.at[pl.ds(own + OV + 2, OV), body],
            zx.at[pl.ds(own, OV), body], zx.at[pl.ds(0, OV), body],
        ),
        NEAR1: (
            z1x.at[1, body], z1x.at[own + 1, body],
            z1x.at[own, body], z1x.at[0, body],
        ),
    }
    for call, key in enumerate((SPILL0, SPILL1)):
        plans[key] = (
            fields.at[1, pl.ds(1, OV), body], spills.at[call, 1],
            fields.at[1, pl.ds(own + OV + 1, OV), body], spills.at[call, 0],
        )

    def remote(key, side):
        peer = me - 1 if side == 0 else me + 1
        return pltpu.make_async_remote_copy(
            src_ref=plans[key][2 * side], dst_ref=plans[key][2 * side + 1],
            send_sem=send_sem.at[key, side], recv_sem=recv_sem.at[key, side],
            device_id={"gx": peer}, device_id_type=MESH,
        )

    has_left, has_right = me > 0, me < n - 1

    def send(key):
        @pl.when(has_left)
        def _():
            remote(key, 0).start()

        @pl.when(has_right)
        def _():
            remote(key, 1).start()

    def received(key):
        @pl.when(has_right)
        def _():
            remote(key, 0).wait_recv()

        @pl.when(has_left)
        def _():
            remote(key, 1).wait_recv()

    def sent(key):
        @pl.when(has_left)
        def _():
            remote(key, 0).wait_send()

        @pl.when(has_right)
        def _():
            remote(key, 1).wait_send()

    def broadcast(slot, row):
        cast[slot, me] = row

        @pl.loop(1, n)
        def _(k):
            pltpu.make_async_remote_copy(
                src_ref=cast.at[slot, me], dst_ref=cast.at[slot, me],
                send_sem=cast_send.at[slot], recv_sem=cast_recv.at[slot],
                device_id={"gx": lax.rem(me + k, n)}, device_id_type=MESH,
            ).start()

    def gathered(slot):
        others = cast.at[slot, pl.ds(0, n - 1)]
        pltpu.make_async_copy(others, others, cast_recv.at[slot]).wait()

    def cast_sent(slot):
        others = cast.at[slot, pl.ds(0, n - 1)]
        pltpu.make_async_copy(others, others, cast_send.at[slot]).wait()

    send(PERM)
    send(RHS)

    def clear(ref, planes):
        zero = jnp.zeros((PAD, nz), F32)
        for plane in range(planes):
            ref[plane, pl.ds(0, PAD), :] = zero
            ref[plane, pl.ds(PAD + ny, PAD), :] = zero

    for half in range(2):
        clear(fields.at[half], wide + 2)
        for plane in (0, wide + 1):
            fields[half, plane, body, :] = jnp.zeros((ny, nz), F32)
    clear(zx, own + 2 * OV + 2)
    clear(z1x, own + 2)
    rows[...] = jnp.zeros(rows.shape, F32)
    kx[pl.ds(OV + 1, own)] = perm_ref[...]
    fx[pl.ds(OV, own)] = src_ref[...]

    @pl.when(jnp.logical_not(has_left))
    def _():
        for plane in range(OV + 1):
            kx[plane] = perm_ref[0]
            zx[plane, body, :] = jnp.zeros((ny, nz), F32)
        fx[pl.ds(0, OV)] = jnp.zeros((OV, ny, nz), F32)
        z1x[0, body, :] = jnp.zeros((ny, nz), F32)
        for call in range(2):
            spills[call, 0] = jnp.zeros((OV, ny, nz), F32)

    @pl.when(jnp.logical_not(has_right))
    def _():
        for plane in range(OV + 1):
            kx[own + OV + 1 + plane] = perm_ref[own - 1]
            zx[own + OV + 1 + plane, body, :] = jnp.zeros((ny, nz), F32)
        fx[pl.ds(own + OV, OV)] = jnp.zeros((OV, ny, nz), F32)
        z1x[own + 1, body, :] = jnp.zeros((ny, nz), F32)
        for call in range(2):
            spills[call, 1] = jnp.zeros((OV, ny, nz), F32)

    for i in range(n):
        block = inverse_ref[:, i * modes:(i + 1) * modes]
        coarse_rows[i] = jnp.concatenate(
            [block, jnp.zeros((modes, nz - modes), F32)], axis=1
        )

    width = width_ref[0]
    extent = extent_ref[0]
    lane = lax.broadcasted_iota(jnp.int32, (1, nz), 1)

    def fold(block):
        return jnp.sum(block.reshape(-1, 8, nz), axis=0)

    def to_row(table):
        ones = jnp.ones((8, nz), F32)
        out = lax.dot_general(
            ones, table, (((1,), (1,)), ((), ())), precision=HIGHEST,
            preferred_element_type=F32,
        )
        return out[0:1]

    def project(f_ref, wait):
        halves = ny // HALF

        @pl.loop(0, groups)
        def _(g):
            if wait:
                basis_copy(g).wait()
            base = g * GROUP

            def step(t, sums):
                plane, start = t // halves, pl.multiple_of((t % halves) * HALF, HALF)
                values = f_ref[OV + plane, pl.ds(start, HALF), :]
                return tuple(
                    sums[j] + fold(basis[base + j, plane, pl.ds(start, HALF), :] * values)
                    for j in range(GROUP)
                )

            sums = lax.fori_loop(
                0, own * halves, step, tuple(jnp.zeros((8, nz), F32) for _ in range(GROUP))
            )
            rows[pl.ds(pl.multiple_of(base, GROUP), GROUP), :] = jnp.concatenate(
                [jnp.sum(s, axis=0, keepdims=True) for s in sums], axis=0
            )

        return jnp.where(lane < width, to_row(rows[...]), 0.0)

    def coarse_solve(slot):
        gathered(slot)

        def step(i, total):
            return total + coarse_rows[i] * cast[slot, i]

        table = lax.fori_loop(0, n, step, jnp.zeros((modes, nz), F32))
        table = jnp.concatenate([table, jnp.zeros((nz - modes, nz), F32)], axis=0)
        broadcast(slot + 1, to_row(table))

    def coarse_spread(slot):
        gathered(slot)

        def step(b, total):
            return total + jnp.where(owner_ref[b] == me, cast[slot, b], 0.0)

        mine = lax.fori_loop(0, n, step, jnp.zeros((1, nz), F32))
        mine = jnp.where(lane < width, mine, 0.0)
        at = lax.broadcasted_iota(jnp.int32, (modes, nz), 0)
        across = lax.broadcasted_iota(jnp.int32, (modes, nz), 1)
        spread[...] = jnp.dot(
            jnp.where(at == across, mine, 0.0), jnp.ones((nz, nz), F32),
            precision=HIGHEST, preferred_element_type=F32,
        )

    def harmonic(left, right):
        return 2.0 * left * right / (left + right)

    def couple(p):
        y_at = lax.broadcasted_iota(jnp.int32, (ny, nz), 0)
        z_at = lax.broadcasted_iota(jnp.int32, (ny, nz), 1)
        centre = kx[p + 1]
        lower_x, upper_x = harmonic(centre, kx[p]), harmonic(centre, kx[p + 2])
        upper_y = jnp.where(
            y_at == ny - 1, centre, harmonic(centre, pltpu.roll(centre, ny - 1, 0))
        )
        lower_y = jnp.where(y_at == 0, centre, pltpu.roll(upper_y, 1, 0))
        upper_z = jnp.where(
            z_at == nz - 1, centre, harmonic(centre, pltpu.roll(centre, nz - 1, 1))
        )
        lower_z = jnp.where(z_at == 0, centre, pltpu.roll(upper_z, 1, 1))
        d = lower_x + upper_x + lower_y + upper_y + lower_z + upper_z
        plane = me * own - OV + p
        inside = (p >= OV - extent) & (p < OV + own + extent)
        inside = inside & (plane >= 0) & (plane < n * own)
        factor = jnp.where(inside, OMEGA, 0.0) / d
        diagonal[p] = d * (1.0 / OMEGA)
        scale[p] = factor
        weights[0, p] = lower_x * factor
        weights[1, p] = upper_x * factor
        weights[2, p] = jnp.where(y_at == 0, 0.0, lower_y * factor)
        weights[3, p] = jnp.where(y_at == ny - 1, 0.0, upper_y * factor)
        weights[4, p] = jnp.where(z_at == 0, 0.0, lower_z * factor)
        weights[5, p] = jnp.where(z_at == nz - 1, 0.0, upper_z * factor)

    def beside(ref, q, p, start, centre):
        here, at = pl.ds(start, ROWS), PAD + start
        total = weights[0, p, here, :] * ref[q - 1, pl.ds(at, ROWS), :]
        total += weights[1, p, here, :] * ref[q + 1, pl.ds(at, ROWS), :]
        total += weights[2, p, here, :] * ref[q, pl.ds(at - 1, ROWS), :]
        total += weights[3, p, here, :] * ref[q, pl.ds(at + 1, ROWS), :]
        total += weights[4, p, here, :] * pltpu.roll(centre, 1, 1)
        total += weights[5, p, here, :] * pltpu.roll(centre, nz - 1, 1)
        return total

    def begin(f_ref, p):
        value = f_ref[p] * scale[p]
        rhs[p] = value
        fields[0, p + 1, body, :] = value

    def sweep_plane(source, target, p):
        for start in range(0, ny, ROWS):
            here = pl.ds(PAD + start, ROWS)
            centre = source[p + 1, here, :]
            target[p + 1, here, :] = (
                rhs[p, pl.ds(start, ROWS), :] + (1.0 - OMEGA) * centre
                + beside(source, p + 1, p, start, centre)
            )

    def sweeps(first, last):
        @pl.loop(first, last)
        def _(s):
            source, target = fields.at[s % 2], fields.at[(s + 1) % 2]

            @pl.loop(0, wide)
            def _(p):
                sweep_plane(source, target, p)

    def apply(ref, q, p, start):
        centre = ref[q, pl.ds(PAD + start, ROWS), :]
        near = beside(ref, q, p, start, centre)
        return centre, diagonal[p, pl.ds(start, ROWS), :] * (OMEGA * centre - near)

    def correct(out_ref, first):
        halves = ny // HALF

        @pl.loop(0, own * halves)
        def _(t):
            plane, start = t // halves, pl.multiple_of((t % halves) * HALF, HALF)
            total = fields[1, OV + 1 + plane, pl.ds(PAD + start, HALF), :]
            for j in range(modes):
                total += spread[j:j + 1, :] * basis[j, plane, pl.ds(start, HALF), :]
            out_ref[first + plane, pl.ds(PAD + start, HALF), :] = total

    def precondition(f_ref, slot, key, call, out_ref, first):
        @pl.loop(0, wide)
        def _(p):
            begin(f_ref, p)

        sweeps(0, 2)
        coarse_solve(slot)
        sweeps(2, SWEEPS - 2)
        source, target = fields.at[0], fields.at[1]

        @pl.loop(0, OV)
        def _(p):
            sweep_plane(source, target, p)
            sweep_plane(source, target, p + own + OV)

        send(key)

        @pl.loop(OV, OV + own)
        def _(p):
            sweep_plane(source, target, p)

        coarse_spread(slot + 1)
        correct(out_ref, first)
        received(key)
        for plane in range(OV):
            out_ref[first + plane, body, :] += spills[call, 0, plane]
        for plane in range(OV):
            out_ref[first + own - OV + plane, body, :] += spills[call, 1, plane]

    def total_of(block):
        return jnp.sum(block, axis=(0, 1), keepdims=True)

    zero = jnp.zeros((8, nz), F32)

    broadcast(0, project(fx, True))
    received(PERM)

    @pl.loop(0, wide)
    def _(p):
        couple(p)

    received(RHS)
    precondition(fx, 0, SPILL0, 0, zx, OV + 1)
    send(NEAR0)
    send(FAR0)
    received(NEAR0)

    def first_image(p, sums):
        rz, za = sums
        for start in range(0, ny, ROWS):
            centre, value = apply(zx, p + 1, p, start)
            vx[p, pl.ds(start, ROWS), :] = value
            rz += fold(centre * fx[p, pl.ds(start, ROWS), :])
            za += fold(centre * value)
        return rz, za

    rz, za = lax.fori_loop(OV, OV + own, first_image, (zero, zero))
    row = project(vx, False)
    row = jnp.where(lane == nz - 2, total_of(rz), row)
    row = jnp.where(lane == nz - 1, total_of(za), row)
    broadcast(2, row)
    received(FAR0)

    @pl.loop(0, OV)
    def _(p):
        for q in (p, p + own + OV):
            for start in range(0, ny, ROWS):
                vx[q, pl.ds(start, ROWS), :] = apply(zx, q + 1, q, start)[1]

    sent(SPILL0)
    precondition(vx, 2, SPILL1, 1, z1x, 1)

    sums = lax.fori_loop(0, n, lambda i, s: s + cast[2, i], jnp.zeros((1, nz), F32))
    rz = total_of(jnp.where(lane == nz - 2, sums, 0.0))
    za = total_of(jnp.where(lane == nz - 1, sums, 0.0))
    step0 = rz / za

    @pl.loop(0, own)
    def _(p):
        z1x[p + 1, body, :] = zx[OV + 1 + p, body, :] - step0 * z1x[p + 1, body, :]

    send(NEAR1)
    received(NEAR1)

    def second_image(p, sums):
        rz1, za1, zv = sums
        for start in range(0, ny, ROWS):
            here = pl.ds(start, ROWS)
            centre, value = apply(z1x, p + 1, p + OV, start)
            image[p, here, :] = value
            before = vx[p + OV, here, :]
            rz1 += fold(centre * (fx[p + OV, here, :] - step0 * before))
            za1 += fold(centre * value)
            zv += fold(centre * before)
        return rz1, za1, zv

    rz1, za1, zv = lax.fori_loop(0, own, second_image, (zero, zero, zero))
    row = jnp.where(lane == 0, total_of(rz1), 0.0)
    row = jnp.where(lane == 1, total_of(za1), row)
    row = jnp.where(lane == 2, total_of(zv), row)
    broadcast(4, row)
    gathered(4)
    sums = lax.fori_loop(0, n, lambda i, s: s + cast[4, i], jnp.zeros((1, nz), F32))
    rz1 = total_of(jnp.where(lane == 0, sums, 0.0))
    za1 = total_of(jnp.where(lane == 1, sums, 0.0))
    zv = total_of(jnp.where(lane == 2, sums, 0.0))
    beta = rz1 / rz
    step1 = rz1 / (za1 + beta * (2.0 * zv + beta * za))
    both = step0 + step1 * beta

    @pl.loop(0, own)
    def _(p):
        pressure_ref[p] = both * zx[OV + 1 + p, body, :] + step1 * z1x[p + 1, body, :]
        residual_ref[p] = fx[OV + p] - both * vx[OV + p] - step1 * image[p]

    for key in (PERM, RHS, NEAR0, FAR0, SPILL1, NEAR1):
        sent(key)
    for slot in range(5):
        cast_sent(slot)


def per_device(n, pressure_source, permeability, basis, widths, extents, coarse_owner, coarse_inverse):
    own, ny, nz = pressure_source.shape
    modes = basis.shape[0]
    wide = own + 2 * OV
    tall = ny + 2 * PAD
    vmem = pl.BlockSpec(memory_space=pltpu.VMEM)
    smem = pl.BlockSpec(memory_space=pltpu.SMEM)
    out = jax.ShapeDtypeStruct((own, ny, nz), F32)
    dma = pltpu.SemaphoreType.DMA
    return pl.pallas_call(
        functools.partial(kernel, n),
        out_shape=(out, out),
        in_specs=[vmem, vmem, smem, smem, smem, vmem, pl.BlockSpec(memory_space=pl.ANY)],
        out_specs=(vmem, vmem),
        scratch_shapes=[
            pltpu.VMEM(basis.shape, F32),
            pltpu.VMEM((wide + 2, ny, nz), F32),
            pltpu.VMEM((wide, ny, nz), F32),
            pltpu.VMEM((wide, ny, nz), F32),
            pltpu.VMEM((6, wide, ny, nz), F32),
            pltpu.VMEM((wide, ny, nz), F32),
            pltpu.VMEM((wide, ny, nz), F32),
            pltpu.VMEM((wide, ny, nz), F32),
            pltpu.VMEM((2, wide + 2, tall, nz), F32),
            pltpu.VMEM((2, 2, OV, ny, nz), F32),
            pltpu.VMEM((wide + 2, tall, nz), F32),
            pltpu.VMEM((own + 2, tall, nz), F32),
            pltpu.VMEM((own, ny, nz), F32),
            pltpu.VMEM((nz, nz), F32),
            pltpu.VMEM((n, modes, nz), F32),
            pltpu.VMEM((modes, nz), F32),
            pltpu.VMEM((5, n, 1, nz), F32),
            dma((modes // GROUP,)),
            dma((7, 2)),
            dma((7, 2)),
            dma((5,)),
            dma((5,)),
        ],
        compiler_params=pltpu.CompilerParams(
            collective_id=0, has_side_effects=True, vmem_limit_bytes=48 * 1024 * 1024
        ),
        name="schwarz_cg",
    )(pressure_source, permeability, widths, extents, coarse_owner, coarse_inverse, basis)


def solution(mesh):
    split = P(("grp", "gx"), None, None)
    placed = (
        split, split, P(None, ("grp", "gx"), None, None),
        P(("grp", "gx")), P(("grp", "gx")), P("grp"), P(("grp", "gx"), None),
    )
    return jax.shard_map(
        functools.partial(per_device, mesh.shape["gx"]),
        mesh=mesh, in_specs=placed, out_specs=(split, split), check_vma=False,
    )
```

time: 387 us -> 64.6 us (0.17); the launches traced: 380 us -> 64.4 us
  blocking collectives: 220 us -> 0 us
  Pallas kernels: 0 us -> 57.6 us
  matrix products: 56.3 us -> 0 us
  other arithmetic: 36.1 us -> 0 us
  starting transfers between devices: 29.3 us -> 0 us
  local copies, waits for them, and re-layouts: 23.1 us -> 4.85 us
  waiting for transfers between devices: 7.35 us -> 0 us
  between operations: 7.24 us -> 1.94 us
    unnamed x4 -> x0, blocking collectives: 125 us -> none
    psum x3 -> x0, blocking collectives: 95.8 us -> none  [the longest x2 65.1 us: residual_product(): return lax.psum(jnp.sum(left * right), 'gx')]
    pallas_call x0 -> x1, Pallas kernels: none -> 57.6 us  [per_device(): pl.pallas_call(functools.partial(kernel, n), out_shape=(out, out), in_spe...]
    dot_general x8 -> x0, matrix products: 56.3 us -> none  [the longest x2 33.5 us: precondition(): jnp.dot(basis_rows, residual_own.reshape(-1), precision=highest)]
    ppermute x14 -> x0, starting transfers between devices: 29.3 us -> none  [the longest x7 20.1 us: with_halo(): lax.ppermute(lax.slice_in_dim(block, block.shape[dim] - width, None, axis...]
    select_n x13 -> x0, other arithmetic: 23.1 us -> none  [the longest x12 23 us: smoother(): jnp.where(inside, update + OMEGA * (rhs_values - action) / couplings[6],...]
    unnamed x41 -> x10, local copies, waits for them, and re-layouts: 19 us -> 4.85 us
    ppermute x14 -> x0, waiting for transfers between devices: 7.35 us -> none  [the longest x7 7.33 us: with_halo(): lax.ppermute(lax.slice_in_dim(block, 0, width, axis=dim), axis, backward)]
  transfers between devices with their start and end apart: 14 -> 0, of which waited for: 4 -> 0; matrix products, arithmetic and copies ran while one was open for 16% -> 0% of each run, Pallas kernels for 0% -> 0%
where the time goes in v1:
time: 64.6 us; the launch traced here: 64.4 us
  Pallas kernels  57.6 us (89%)
  local copies, waits for them, and re-layouts  4.85 us (8%)
  between operations  1.94 us (3%)
    pallas_call x1, Pallas kernels, per_device(): pl.pallas_call(functools.partial(kernel, n), out_shape=(out, out), in_spe...  57.6 us
    unnamed x10, local copies, waits for them, and re-layouts  4.85 us

profile of v1, /device:TPU:0, one launch (start us, length us, event | category | flops | bytes accessed | tf_op | source)
XLA Modules:
  0.0 64.4 jit_solution(14290430935678206831)
XLA Ops:
  1.9 0.0 copy-start
  1.9 0.9 %copy-done = f32[4,128,128]{2,1,0:T(8,128)S(1)} copy-done((f32[4,128,128]{2,1,0:T(8,128)S(1)}, f32[4,128,128]{2,1,0:T(8,128)}, u32[]{:S(2)}) %copy-start) | copy-done | bytes 262168
  2.9 0.0 copy-start.1
  2.9 0.9 %copy-done.1 = f32[4,128,128]{2,1,0:T(8,128)S(1)} copy-done((f32[4,128,128]{2,1,0:T(8,128)S(1)}, f32[4,128,128]{2,1,0:T(8,128)}, u32[]{:S(2)}) %copy-start.1) | copy-done | bytes 262168
  3.8 0.0 copy-start.2
  3.8 0.9 %copy-done.2 = f32[40,640]{1,0:T(8,128)S(1)} copy-done((f32[40,640]{1,0:T(8,128)S(1)}, f32[40,640]{1,0:T(8,128)}, u32[]{:S(2)}) %copy-start.2) | copy-done | bytes 102424
  4.7 0.0 copy-start.3
  4.7 0.7 %copy-done.3 = s32[16]{0:T(128)S(1)} copy-done((s32[16]{0:T(128)S(1)}, s32[16]{0:T(128)}, u32[]{:S(2)}) %copy-start.3) | copy-done | bytes 88
  5.4 57.6 %schwarz_cg.1 = (f32[4,128,128]{2,1,0:T(8,128)S(1)}, f32[4,128,128]{2,1,0:T(8,128)S(1)}) custom-call(f32[4,128,128]{2,1,0:T(8,128)S(1)} %copy-done, f32[4,128,128]{2,1,0:T(8,128)S(1)} %copy-done.1, s32[1]{0:T(128)S(6)} %copy.11.width_ref, s32[1]{0:T(128)S(6)} %copy.12.extent_ref, s32[16]{0:T(128)S(1)} %copy-done.3, f32[40,640]{1,0:T(8,128)S(1)} %copy-done.2, ...), custom_call_target="tpu_custom_call" | custom-call | tf_op jit(solution)/shard_map/schwarz_cg/pallas_call | solution.py:457
  63.0 0.7 %copy.13 = f32[4,128,128]{2,1,0:T(8,128)} copy(f32[4,128,128]{2,1,0:T(8,128)S(1)} %get-tuple-element.4) | data formatting | bytes 524288
  63.7 0.7 %copy.14 = f32[4,128,128]{2,1,0:T(8,128)} copy(f32[4,128,128]{2,1,0:T(8,128)S(1)} %get-tuple-element.5) | data formatting | bytes 524288
Async XLA Ops:
  1.9 1.0 %copy-start = (f32[4,128,128]{2,1,0:T(8,128)S(1)}, f32[4,128,128]{2,1,0:T(8,128)}, u32[]{:S(2)}) copy-start(f32[4,128,128]{2,1,0:T(8,128)} %src_ref.1) | copy-start | bytes 786436
  2.9 0.9 %copy-start.1 = (f32[4,128,128]{2,1,0:T(8,128)S(1)}, f32[4,128,128]{2,1,0:T(8,128)}, u32[]{:S(2)}) copy-start(f32[4,128,128]{2,1,0:T(8,128)} %perm_ref.1) | copy-start | bytes 786436
  3.8 0.9 %copy-start.2 = (f32[40,640]{1,0:T(8,128)S(1)}, f32[40,640]{1,0:T(8,128)}, u32[]{:S(2)}) copy-start(f32[40,640]{1,0:T(8,128)} %inverse_ref.1) | copy-start | bytes 307204
  4.7 0.7 %copy-start.3 = (s32[16]{0:T(128)S(1)}, s32[16]{0:T(128)}, u32[]{:S(2)}) copy-start(s32[16]{0:T(128)} %owner_ref.1) | copy-start | bytes 196

commit v2 on v1

--- a/solution.py
+++ b/solution.py
@@ -21,13 +21,16 @@
 
 
 def kernel(
-    n, src_ref, perm_ref, width_ref, extent_ref, owner_ref, inverse_ref, basis_ref,
+    n, src_hbm, perm_hbm, width_hbm, extent_hbm, owner_hbm, inverse_hbm, basis_ref,
     pressure_ref, residual_ref,
     basis, kx, fx, vx, weights, scale, diagonal, rhs, fields, spills, zx, z1x, image,
-    rows, coarse_rows, spread, cast, basis_sem, send_sem, recv_sem, cast_send, cast_recv,
+    rows, coarse_rows, spread, cast, kp, fp, flat, inverse_ref,
+    width_ref, extent_ref, owner_ref,
+    basis_sem, send_sem, recv_sem, cast_send, cast_recv, load_sem,
 ):
     me = lax.axis_index("gx")
-    own, ny, nz = src_ref.shape
+    own, ny, nz = src_hbm.shape
+    tall = ny // 8
     wide = own + 2 * OV
     modes = basis_ref.shape[0]
     groups = modes // GROUP
@@ -36,6 +39,16 @@
         part = pl.ds(g * GROUP, GROUP)
         return pltpu.make_async_copy(basis_ref.at[part], basis.at[part], basis_sem.at[g])
 
+    loads = [
+        pltpu.make_async_copy(source, target, load_sem.at[i])
+        for i, (source, target) in enumerate((
+            (perm_hbm, kx.at[pl.ds(OV + 1, own)]), (src_hbm, fx.at[pl.ds(OV, own)]),
+            (width_hbm, width_ref), (extent_hbm, extent_ref), (owner_hbm, owner_ref),
+            (inverse_hbm, inverse_ref),
+        ))
+    ]
+    for load in loads:
+        load.start()
     for g in range(groups):
         basis_copy(g).start()
 
@@ -52,12 +65,12 @@
     body = pl.ds(PAD, ny)
     plans = {
         PERM: (
-            perm_ref.at[pl.ds(0, OV + 1)], kx.at[pl.ds(own + OV + 1, OV + 1)],
-            perm_ref.at[pl.ds(own - OV - 1, OV + 1)], kx.at[pl.ds(0, OV + 1)],
+            kx.at[pl.ds(OV + 1, OV + 1)], kx.at[pl.ds(own + OV + 1, OV + 1)],
+            kx.at[pl.ds(own, OV + 1)], kx.at[pl.ds(0, OV + 1)],
         ),
         RHS: (
-            src_ref.at[pl.ds(0, OV)], fx.at[pl.ds(own + OV, OV)],
-            src_ref.at[pl.ds(own - OV, OV)], fx.at[pl.ds(0, OV)],
+            fx.at[pl.ds(OV, OV)], fx.at[pl.ds(own + OV, OV)],
+            fx.at[pl.ds(own, OV)], fx.at[pl.ds(0, OV)],
         ),
         NEAR0: (
             zx.at[OV + 1, body], zx.at[own + OV + 1, body],
@@ -134,29 +147,20 @@
         others = cast.at[slot, pl.ds(0, n - 1)]
         pltpu.make_async_copy(others, others, cast_send.at[slot]).wait()
 
+    loads[0].wait()
     send(PERM)
+    loads[1].wait()
     send(RHS)
 
-    def clear(ref, planes):
-        zero = jnp.zeros((PAD, nz), F32)
-        for plane in range(planes):
-            ref[plane, pl.ds(0, PAD), :] = zero
-            ref[plane, pl.ds(PAD + ny, PAD), :] = zero
-
     for half in range(2):
-        clear(fields.at[half], wide + 2)
         for plane in (0, wide + 1):
             fields[half, plane, body, :] = jnp.zeros((ny, nz), F32)
-    clear(zx, own + 2 * OV + 2)
-    clear(z1x, own + 2)
     rows[...] = jnp.zeros(rows.shape, F32)
-    kx[pl.ds(OV + 1, own)] = perm_ref[...]
-    fx[pl.ds(OV, own)] = src_ref[...]
 
     @pl.when(jnp.logical_not(has_left))
     def _():
         for plane in range(OV + 1):
-            kx[plane] = perm_ref[0]
+            kx[plane] = kx[OV + 1]
             zx[plane, body, :] = jnp.zeros((ny, nz), F32)
         fx[pl.ds(0, OV)] = jnp.zeros((OV, ny, nz), F32)
         z1x[0, body, :] = jnp.zeros((ny, nz), F32)
@@ -166,13 +170,15 @@
     @pl.when(jnp.logical_not(has_right))
     def _():
         for plane in range(OV + 1):
-            kx[own + OV + 1 + plane] = perm_ref[own - 1]
+            kx[own + OV + 1 + plane] = kx[own + OV]
             zx[own + OV + 1 + plane, body, :] = jnp.zeros((ny, nz), F32)
         fx[pl.ds(own + OV, OV)] = jnp.zeros((OV, ny, nz), F32)
         z1x[own + 1, body, :] = jnp.zeros((ny, nz), F32)
         for call in range(2):
             spills[call, 1] = jnp.zeros((OV, ny, nz), F32)
 
+    for load in loads[2:]:
+        load.wait()
     for i in range(n):
         block = inverse_ref[:, i * modes:(i + 1) * modes]
         coarse_rows[i] = jnp.concatenate(
@@ -194,7 +200,7 @@
         )
         return out[0:1]
 
-    def project(f_ref, wait):
+    def project(f_ref, first, wait):
         halves = ny // HALF
 
         @pl.loop(0, groups)
@@ -205,7 +211,7 @@
 
             def step(t, sums):
                 plane, start = t // halves, pl.multiple_of((t % halves) * HALF, HALF)
-                values = f_ref[OV + plane, pl.ds(start, HALF), :]
+                values = f_ref[first + plane, pl.ds(start, HALF), :]
                 return tuple(
                     sums[j] + fold(basis[base + j, plane, pl.ds(start, HALF), :] * values)
                     for j in range(GROUP)
@@ -248,39 +254,60 @@
     def harmonic(left, right):
         return 2.0 * left * right / (left + right)
 
+    def reorder(source, q, target, p, first):
+        for t in range(tall):
+            target[p, pl.ds(first + 8 * t, 8), :] = source[q, pl.ds(t, 8, stride=tall), :]
+
+    def restore(source, q, target, p):
+        for t in range(tall):
+            target[p, pl.ds(t, 8, stride=tall), :] = source[q, pl.ds(8 * t, 8), :]
+
+    def wrap(ref, q):
+        ref[q, pl.ds(0, 8), :] = pltpu.roll(ref[q, pl.ds(PAD + ny - 8, 8), :], 1, 0)
+        ref[q, pl.ds(PAD + ny, 8), :] = pltpu.roll(ref[q, pl.ds(PAD, 8), :], 7, 0)
+
+    def order_couplings(p):
+        reorder(kx, p, kp, p, PAD)
+        at = lax.broadcasted_iota(jnp.int32, (8, nz), 0)
+        head, tail = kp[p, pl.ds(PAD, 8), :], kp[p, pl.ds(PAD + ny - 8, 8), :]
+        kp[p, pl.ds(0, 8), :] = jnp.where(at == 0, head, pltpu.roll(tail, 1, 0))
+        kp[p, pl.ds(PAD + ny, 8), :] = jnp.where(at == 7, tail, pltpu.roll(head, 7, 0))
+
     def couple(p):
-        y_at = lax.broadcasted_iota(jnp.int32, (ny, nz), 0)
-        z_at = lax.broadcasted_iota(jnp.int32, (ny, nz), 1)
-        centre = kx[p + 1]
-        lower_x, upper_x = harmonic(centre, kx[p]), harmonic(centre, kx[p + 2])
-        upper_y = jnp.where(
-            y_at == ny - 1, centre, harmonic(centre, pltpu.roll(centre, ny - 1, 0))
-        )
-        lower_y = jnp.where(y_at == 0, centre, pltpu.roll(upper_y, 1, 0))
-        upper_z = jnp.where(
-            z_at == nz - 1, centre, harmonic(centre, pltpu.roll(centre, nz - 1, 1))
-        )
-        lower_z = jnp.where(z_at == 0, centre, pltpu.roll(upper_z, 1, 1))
-        d = lower_x + upper_x + lower_y + upper_y + lower_z + upper_z
         plane = me * own - OV + p
         inside = (p >= OV - extent) & (p < OV + own + extent)
         inside = inside & (plane >= 0) & (plane < n * own)
-        factor = jnp.where(inside, OMEGA, 0.0) / d
-        diagonal[p] = d * (1.0 / OMEGA)
-        scale[p] = factor
-        weights[0, p] = lower_x * factor
-        weights[1, p] = upper_x * factor
-        weights[2, p] = jnp.where(y_at == 0, 0.0, lower_y * factor)
-        weights[3, p] = jnp.where(y_at == ny - 1, 0.0, upper_y * factor)
-        weights[4, p] = jnp.where(z_at == 0, 0.0, lower_z * factor)
-        weights[5, p] = jnp.where(z_at == nz - 1, 0.0, upper_z * factor)
+        omega = jnp.where(inside, OMEGA, 0.0)
+        z_at = lax.broadcasted_iota(jnp.int32, (ROWS, nz), 1)
+        for start in range(0, ny, ROWS):
+            y_at = start + lax.broadcasted_iota(jnp.int32, (ROWS, nz), 0)
+            here, at = pl.ds(start, ROWS), PAD + start
+            centre = kp[p + 1, pl.ds(at, ROWS), :]
+            lower_x = harmonic(centre, kp[p, pl.ds(at, ROWS), :])
+            upper_x = harmonic(centre, kp[p + 2, pl.ds(at, ROWS), :])
+            lower_y = harmonic(centre, kp[p + 1, pl.ds(at - 8, ROWS), :])
+            upper_y = harmonic(centre, kp[p + 1, pl.ds(at + 8, ROWS), :])
+            upper_z = jnp.where(
+                z_at == nz - 1, centre, harmonic(centre, pltpu.roll(centre, nz - 1, 1))
+            )
+            lower_z = jnp.where(z_at == 0, centre, pltpu.roll(upper_z, 1, 1))
+            d = lower_x + upper_x + lower_y + upper_y + lower_z + upper_z
+            factor = omega / d
+            diagonal[p, here, :] = d * (1.0 / OMEGA)
+            scale[p, here, :] = factor
+            weights[0, p, here, :] = lower_x * factor
+            weights[1, p, here, :] = upper_x * factor
+            weights[2, p, here, :] = jnp.where(y_at == 0, 0.0, lower_y * factor)
+            weights[3, p, here, :] = jnp.where(y_at == ny - 1, 0.0, upper_y * factor)
+            weights[4, p, here, :] = jnp.where(z_at == 0, 0.0, lower_z * factor)
+            weights[5, p, here, :] = jnp.where(z_at == nz - 1, 0.0, upper_z * factor)
 
     def beside(ref, q, p, start, centre):
         here, at = pl.ds(start, ROWS), PAD + start
         total = weights[0, p, here, :] * ref[q - 1, pl.ds(at, ROWS), :]
         total += weights[1, p, here, :] * ref[q + 1, pl.ds(at, ROWS), :]
-        total += weights[2, p, here, :] * ref[q, pl.ds(at - 1, ROWS), :]
-        total += weights[3, p, here, :] * ref[q, pl.ds(at + 1, ROWS), :]
+        total += weights[2, p, here, :] * ref[q, pl.ds(at - 8, ROWS), :]
+        total += weights[3, p, here, :] * ref[q, pl.ds(at + 8, ROWS), :]
         total += weights[4, p, here, :] * pltpu.roll(centre, 1, 1)
         total += weights[5, p, here, :] * pltpu.roll(centre, nz - 1, 1)
         return total
@@ -289,6 +316,7 @@
         value = f_ref[p] * scale[p]
         rhs[p] = value
         fields[0, p + 1, body, :] = value
+        wrap(fields.at[0], p + 1)
 
     def sweep_plane(source, target, p):
         for start in range(0, ny, ROWS):
@@ -298,6 +326,7 @@
                 rhs[p, pl.ds(start, ROWS), :] + (1.0 - OMEGA) * centre
                 + beside(source, p + 1, p, start, centre)
             )
+        wrap(target, p + 1)
 
     def sweeps(first, last):
         @pl.loop(first, last)
@@ -313,16 +342,28 @@
         near = beside(ref, q, p, start, centre)
         return centre, diagonal[p, pl.ds(start, ROWS), :] * (OMEGA * centre - near)
 
-    def correct(out_ref, first):
+    def correct():
         halves = ny // HALF
 
         @pl.loop(0, own * halves)
         def _(t):
             plane, start = t // halves, pl.multiple_of((t % halves) * HALF, HALF)
-            total = fields[1, OV + 1 + plane, pl.ds(PAD + start, HALF), :]
+            total = jnp.zeros((HALF, nz), F32)
             for j in range(modes):
                 total += spread[j:j + 1, :] * basis[j, plane, pl.ds(start, HALF), :]
-            out_ref[first + plane, pl.ds(PAD + start, HALF), :] = total
+            flat[plane, pl.ds(start, HALF), :] = total
+
+    def gather_parts(call, out_ref, first):
+        for plane in range(own):
+            for t in range(tall):
+                here = pl.ds(8 * t, 8)
+                total = fields[1, OV + 1 + plane, pl.ds(PAD + 8 * t, 8), :]
+                total += flat[plane, pl.ds(t, 8, stride=tall), :]
+                if plane < OV:
+                    total += spills[call, 0, plane, here, :]
+                if plane >= own - OV:
+                    total += spills[call, 1, plane - own + OV, here, :]
+                out_ref[first + plane, pl.ds(PAD + 8 * t, 8), :] = total
 
     def precondition(f_ref, slot, key, call, out_ref, first):
         @pl.loop(0, wide)
@@ -346,42 +387,53 @@
             sweep_plane(source, target, p)
 
         coarse_spread(slot + 1)
-        correct(out_ref, first)
+        correct()
         received(key)
-        for plane in range(OV):
-            out_ref[first + plane, body, :] += spills[call, 0, plane]
-        for plane in range(OV):
-            out_ref[first + own - OV + plane, body, :] += spills[call, 1, plane]
+        gather_parts(call, out_ref, first)
 
     def total_of(block):
         return jnp.sum(block, axis=(0, 1), keepdims=True)
 
     zero = jnp.zeros((8, nz), F32)
 
-    broadcast(0, project(fx, True))
+    broadcast(0, project(fx, OV, True))
     received(PERM)
 
+    @pl.loop(0, wide + 2)
+    def _(p):
+        order_couplings(p)
+
     @pl.loop(0, wide)
     def _(p):
         couple(p)
 
     received(RHS)
-    precondition(fx, 0, SPILL0, 0, zx, OV + 1)
+
+    @pl.loop(0, wide)
+    def _(p):
+        reorder(fx, p, fp, p, 0)
+
+    precondition(fp, 0, SPILL0, 0, zx, OV + 1)
     send(NEAR0)
     send(FAR0)
     received(NEAR0)
+
+    @pl.loop(OV, own + OV + 2)
+    def _(p):
+        wrap(zx, p)
 
     def first_image(p, sums):
         rz, za = sums
         for start in range(0, ny, ROWS):
             centre, value = apply(zx, p + 1, p, start)
             vx[p, pl.ds(start, ROWS), :] = value
-            rz += fold(centre * fx[p, pl.ds(start, ROWS), :])
+            rz += fold(centre * fp[p, pl.ds(start, ROWS), :])
             za += fold(centre * value)
+        restore(vx, p, flat, p - OV)
         return rz, za
 
     rz, za = lax.fori_loop(OV, OV + own, first_image, (zero, zero))
-    row = project(vx, False)
+    row = project(flat, 0, False)
     row = jnp.where(lane == nz - 2, total_of(rz), row)
     row = jnp.where(lane == nz - 1, total_of(za), row)
     broadcast(2, row)
@@ -389,6 +441,11 @@
 
     @pl.loop(0, OV)
     def _(p):
+        wrap(zx, p)
+        wrap(zx, p + own + OV + 2)
+
+    @pl.loop(0, OV)
+    def _(p):
         for q in (p, p + own + OV):
             for start in range(0, ny, ROWS):
                 vx[q, pl.ds(start, ROWS), :] = apply(zx, q + 1, q, start)[1]
@@ -407,6 +464,10 @@
 
     send(NEAR1)
     received(NEAR1)
+
+    @pl.loop(0, own + 2)
+    def _(p):
+        wrap(z1x, p)
 
     def second_image(p, sums):
         rz1, za1, zv = sums
@@ -415,7 +476,7 @@
             centre, value = apply(z1x, p + 1, p + OV, start)
             image[p, here, :] = value
             before = vx[p + OV, here, :]
-            rz1 += fold(centre * (fx[p + OV, here, :] - step0 * before))
+            rz1 += fold(centre * (fp[p + OV, here, :] - step0 * before))
             za1 += fold(centre * value)
             zv += fold(centre * before)
         return rz1, za1, zv
@@ -436,8 +497,12 @@
 
     @pl.loop(0, own)
     def _(p):
-        pressure_ref[p] = both * zx[OV + 1 + p, body, :] + step1 * z1x[p + 1, body, :]
-        residual_ref[p] = fx[OV + p] - both * vx[OV + p] - step1 * image[p]
+        for t in range(tall):
+            here, at, place = pl.ds(8 * t, 8), pl.ds(PAD + 8 * t, 8), pl.ds(t, 8, stride=tall)
+            pressure_ref[p, place, :] = both * zx[OV + 1 + p, at, :] + step1 * z1x[p + 1, at, :]
+            residual_ref[p, place, :] = (
+                fp[OV + p, here, :] - both * vx[OV + p, here, :] - step1 * image[p, here, :]
+            )
 
     for key in (PERM, RHS, NEAR0, FAR0, SPILL1, NEAR1):
         sent(key)
@@ -451,13 +516,14 @@
     wide = own + 2 * OV
     tall = ny + 2 * PAD
     vmem = pl.BlockSpec(memory_space=pltpu.VMEM)
-    smem = pl.BlockSpec(memory_space=pltpu.SMEM)
+    hbm = pl.BlockSpec(memory_space=pl.ANY)
+    smem = pltpu.SMEM
     out = jax.ShapeDtypeStruct((own, ny, nz), F32)
     dma = pltpu.SemaphoreType.DMA
     return pl.pallas_call(
         functools.partial(kernel, n),
         out_shape=(out, out),
-        in_specs=[vmem, vmem, smem, smem, smem, vmem, pl.BlockSpec(memory_space=pl.ANY)],
+        in_specs=[hbm] * 7,
         out_specs=(vmem, vmem),
         scratch_shapes=[
             pltpu.VMEM(basis.shape, F32),
@@ -477,11 +543,19 @@
             pltpu.VMEM((n, modes, nz), F32),
             pltpu.VMEM((modes, nz), F32),
             pltpu.VMEM((5, n, 1, nz), F32),
+            pltpu.VMEM((wide + 2, tall, nz), F32),
+            pltpu.VMEM((wide, ny, nz), F32),
+            pltpu.VMEM((own, ny, nz), F32),
+            pltpu.VMEM(coarse_inverse.shape, F32),
+            smem(widths.shape, jnp.int32),
+            smem(extents.shape, jnp.int32),
+            smem(coarse_owner.shape, jnp.int32),
             dma((modes // GROUP,)),
             dma((7, 2)),
             dma((7, 2)),
             dma((5,)),
             dma((5,)),
+            dma((6,)),
         ],
         compiler_params=pltpu.CompilerParams(
             collective_id=0, has_side_effects=True, vmem_limit_bytes=48 * 1024 * 1024

time: 64.6 us -> 65 us (level)
  no operation moved by 1% of the time
where the time goes in v2:
time: 65 us; the launch traced here: 64.8 us
  Pallas kernels  58 us (89%)
  local copies, waits for them, and re-layouts  4.85 us (7%)
  between operations  1.94 us (3%)
    pallas_call x1, Pallas kernels, per_device(): pl.pallas_call(functools.partial(kernel, n), out_shape=(out, out), in_spe...  58 us
    unnamed x10, local copies, waits for them, and re-layouts  4.85 us

profile of v2, /device:TPU:0, one launch (start us, length us, event | category | flops | bytes accessed | tf_op | source)
XLA Modules:
  0.0 64.8 jit_solution(10446122961696643244)
XLA Ops:
  1.9 0.0 copy-start
  1.9 0.9 %copy-done = f32[4,128,128]{2,1,0:T(8,128)S(1)} copy-done((f32[4,128,128]{2,1,0:T(8,128)S(1)}, f32[4,128,128]{2,1,0:T(8,128)}, u32[]{:S(2)}) %copy-start) | copy-done | bytes 262168
  2.9 0.0 copy-start.1
  2.9 0.9 %copy-done.1 = f32[4,128,128]{2,1,0:T(8,128)S(1)} copy-done((f32[4,128,128]{2,1,0:T(8,128)S(1)}, f32[4,128,128]{2,1,0:T(8,128)}, u32[]{:S(2)}) %copy-start.1) | copy-done | bytes 262168
  3.8 0.0 copy-start.2
  3.8 0.9 %copy-done.2 = f32[40,640]{1,0:T(8,128)S(1)} copy-done((f32[40,640]{1,0:T(8,128)S(1)}, f32[40,640]{1,0:T(8,128)}, u32[]{:S(2)}) %copy-start.2) | copy-done | bytes 102424
  4.7 0.0 copy-start.3
  4.7 0.7 %copy-done.3 = s32[16]{0:T(128)S(1)} copy-done((s32[16]{0:T(128)S(1)}, s32[16]{0:T(128)}, u32[]{:S(2)}) %copy-start.3) | copy-done | bytes 88
  5.4 58.0 %schwarz_cg.1 = (f32[4,128,128]{2,1,0:T(8,128)S(1)}, f32[4,128,128]{2,1,0:T(8,128)S(1)}) custom-call(f32[4,128,128]{2,1,0:T(8,128)S(1)} %copy-done, f32[4,128,128]{2,1,0:T(8,128)S(1)} %copy-done.1, s32[1]{0:T(128)S(6)} %copy.11.width_hbm, s32[1]{0:T(128)S(6)} %copy.12.extent_hbm, s32[16]{0:T(128)S(1)} %copy-done.3, f32[40,640]{1,0:T(8,128)S(1)} %copy-done.2, ...), custom_call_target="tpu_custom_call" | custom-call | tf_op jit(solution)/shard_map/schwarz_cg/pallas_call | solution.py:523
  63.4 0.7 %copy.13 = f32[4,128,128]{2,1,0:T(8,128)} copy(f32[4,128,128]{2,1,0:T(8,128)S(1)} %get-tuple-element.4) | data formatting | bytes 524288
  64.1 0.7 %copy.14 = f32[4,128,128]{2,1,0:T(8,128)} copy(f32[4,128,128]{2,1,0:T(8,128)S(1)} %get-tuple-element.5) | data formatting | bytes 524288
Async XLA Ops:
  1.9 1.0 %copy-start = (f32[4,128,128]{2,1,0:T(8,128)S(1)}, f32[4,128,128]{2,1,0:T(8,128)}, u32[]{:S(2)}) copy-start(f32[4,128,128]{2,1,0:T(8,128)} %src_hbm.1) | copy-start | bytes 786436
  2.9 0.9 %copy-start.1 = (f32[4,128,128]{2,1,0:T(8,128)S(1)}, f32[4,128,128]{2,1,0:T(8,128)}, u32[]{:S(2)}) copy-start(f32[4,128,128]{2,1,0:T(8,128)} %perm_hbm.1) | copy-start | bytes 786436
  3.8 0.9 %copy-start.2 = (f32[40,640]{1,0:T(8,128)S(1)}, f32[40,640]{1,0:T(8,128)}, u32[]{:S(2)}) copy-start(f32[40,640]{1,0:T(8,128)} %inverse_hbm.1) | copy-start | bytes 307204
  4.7 0.7 %copy-start.3 = (s32[16]{0:T(128)S(1)}, s32[16]{0:T(128)}, u32[]{:S(2)}) copy-start(s32[16]{0:T(128)} %owner_hbm.1) | copy-start | bytes 196

commit v3 on v2

--- a/solution.py
+++ b/solution.py
@@ -11,6 +11,7 @@
 SWEEPS = 6
 OMEGA = 0.8
 PAD = 8
+UNROLL = 4
 ROWS = 32
 HALF = 64
 GROUP = 8
@@ -23,7 +24,7 @@
 def kernel(
     n, src_hbm, perm_hbm, width_hbm, extent_hbm, owner_hbm, inverse_hbm, basis_ref,
     pressure_ref, residual_ref,
-    basis, kx, fx, vx, weights, scale, diagonal, rhs, fields, spills, zx, z1x, image,
+    basis, kx, fx, vx, weights, scale, diagonal, rhs, even, odd, spills, zx, z1x, image,
     rows, coarse_rows, spread, cast, kp, fp, flat, inverse_ref,
     width_ref, extent_ref, owner_ref,
     basis_sem, send_sem, recv_sem, cast_send, cast_recv, load_sem,
@@ -87,8 +88,8 @@
     }
     for call, key in enumerate((SPILL0, SPILL1)):
         plans[key] = (
-            fields.at[1, pl.ds(1, OV), body], spills.at[call, 1],
-            fields.at[1, pl.ds(own + OV + 1, OV), body], spills.at[call, 0],
+            odd.at[pl.ds(1, OV), body], spills.at[call, 1],
+            odd.at[pl.ds(own + OV + 1, OV), body], spills.at[call, 0],
         )
 
     def remote(key, side):
@@ -152,9 +153,9 @@
     loads[1].wait()
     send(RHS)
 
-    for half in range(2):
+    for half in (even, odd):
         for plane in (0, wide + 1):
-            fields[half, plane, body, :] = jnp.zeros((ny, nz), F32)
+            half[plane, body, :] = jnp.zeros((ny, nz), F32)
     rows[...] = jnp.zeros(rows.shape, F32)
 
     @pl.when(jnp.logical_not(has_left))
@@ -315,27 +316,29 @@
     def begin(f_ref, p):
         value = f_ref[p] * scale[p]
         rhs[p] = value
-        fields[0, p + 1, body, :] = value
-        wrap(fields.at[0], p + 1)
+        even[p + 1, body, :] = value
+        even[p + 1, pl.ds(0, 8), :] = pltpu.roll(value[-8:], 1, 0)
+        even[p + 1, pl.ds(PAD + ny, 8), :] = pltpu.roll(value[:8], 7, 0)
 
     def sweep_plane(source, target, p):
         for start in range(0, ny, ROWS):
             here = pl.ds(PAD + start, ROWS)
             centre = source[p + 1, here, :]
-            target[p + 1, here, :] = (
+            value = (
                 rhs[p, pl.ds(start, ROWS), :] + (1.0 - OMEGA) * centre
                 + beside(source, p + 1, p, start, centre)
             )
-        wrap(target, p + 1)
-
-    def sweeps(first, last):
-        @pl.loop(first, last)
-        def _(s):
-            source, target = fields.at[s % 2], fields.at[(s + 1) % 2]
-
-            @pl.loop(0, wide)
-            def _(p):
-                sweep_plane(source, target, p)
+            target[p + 1, here, :] = value
+            if start == 0:
+                target[p + 1, pl.ds(PAD + ny, 8), :] = pltpu.roll(value[:8], 7, 0)
+            if start == ny - ROWS:
+                target[p + 1, pl.ds(0, 8), :] = pltpu.roll(value[-8:], 1, 0)
+
+    def sweep(source, target):
+        @pl.loop(0, wide, step=UNROLL)
+        def _(p):
+            for more in range(UNROLL):
+                sweep_plane(source, target, p + more)
 
     def apply(ref, q, p, start):
         centre = ref[q, pl.ds(PAD + start, ROWS), :]
@@ -353,43 +356,37 @@
                 total += spread[j:j + 1, :] * basis[j, plane, pl.ds(start, HALF), :]
             flat[plane, pl.ds(start, HALF), :] = total
 
-    def gather_parts(call, out_ref, first):
-        for plane in range(own):
-            for t in range(tall):
-                here = pl.ds(8 * t, 8)
-                total = fields[1, OV + 1 + plane, pl.ds(PAD + 8 * t, 8), :]
-                total += flat[plane, pl.ds(t, 8, stride=tall), :]
-                if plane < OV:
-                    total += spills[call, 0, plane, here, :]
-                if plane >= own - OV:
-                    total += spills[call, 1, plane - own + OV, here, :]
-                out_ref[first + plane, pl.ds(PAD + 8 * t, 8), :] = total
-
-    def precondition(f_ref, slot, key, call, out_ref, first):
-        @pl.loop(0, wide)
+    def gather_part(call, out_ref, first, plane):
+        for t in range(tall):
+            here = pl.ds(8 * t, 8)
+            total = odd[OV + 1 + plane, pl.ds(PAD + 8 * t, 8), :]
+            total += flat[plane, pl.ds(t, 8, stride=tall), :]
+            if plane < OV:
+                total += spills[call, 0, plane, here, :]
+            if plane >= own - OV:
+                total += spills[call, 1, plane - own + OV, here, :]
+            out_ref[first + plane, pl.ds(PAD + 8 * t, 8), :] = total
+
+    def precondition(f_ref, slot, key):
+        @pl.loop(0, wide, step=UNROLL)
         def _(p):
-            begin(f_ref, p)
-
-        sweeps(0, 2)
+            for more in range(UNROLL):
+                begin(f_ref, p + more)
+
+        sweep(even, odd)
+        sweep(odd, even)
         coarse_solve(slot)
-        sweeps(2, SWEEPS - 2)
-        source, target = fields.at[0], fields.at[1]
-
-        @pl.loop(0, OV)
-        def _(p):
-            sweep_plane(source, target, p)
-            sweep_plane(source, target, p + own + OV)
-
+        sweep(even, odd)
+        sweep(odd, even)
+        for p in range(OV):
+            sweep_plane(even, odd, p)
+            sweep_plane(even, odd, p + own + OV)
         send(key)
-
-        @pl.loop(OV, OV + own)
-        def _(p):
-            sweep_plane(source, target, p)
-
+        for p in range(OV, OV + own):
+            sweep_plane(even, odd, p)
         coarse_spread(slot + 1)
         correct()
         received(key)
-        gather_parts(call, out_ref, first)
 
     def total_of(block):
         return jnp.sum(block, axis=(0, 1), keepdims=True)
@@ -413,14 +410,14 @@
     def _(p):
         reorder(fx, p, fp, p, 0)
 
-    precondition(fp, 0, SPILL0, 0, zx, OV + 1)
+    precondition(fp, 0, SPILL0)
+    ends, middle = (0, own - 1), range(1, own - 1)
+    for plane in ends:
+        gather_part(0, zx, OV + 1, plane)
     send(NEAR0)
+    for plane in middle:
+        gather_part(0, zx, OV + 1, plane)
     send(FAR0)
-    received(NEAR0)
-
-    @pl.loop(OV, own + OV + 2)
-    def _(p):
-        wrap(zx, p)
 
     def first_image(p, sums):
         rz, za = sums
@@ -432,42 +429,38 @@
         restore(vx, p, flat, p - OV)
         return rz, za
 
-    rz, za = lax.fori_loop(OV, OV + own, first_image, (zero, zero))
+    sums = (zero, zero)
+    for plane in range(own):
+        wrap(zx, OV + 1 + plane)
+    for plane in middle:
+        sums = first_image(OV + plane, sums)
+    received(NEAR0)
+    for plane in ends:
+        sums = first_image(OV + plane, sums)
+    rz, za = sums
     row = project(flat, 0, False)
     row = jnp.where(lane == nz - 2, total_of(rz), row)
     row = jnp.where(lane == nz - 1, total_of(za), row)
     broadcast(2, row)
     received(FAR0)
-
-    @pl.loop(0, OV)
-    def _(p):
-        wrap(zx, p)
-        wrap(zx, p + own + OV + 2)
-
-    @pl.loop(0, OV)
-    def _(p):
-        for q in (p, p + own + OV):
-            for start in range(0, ny, ROWS):
-                vx[q, pl.ds(start, ROWS), :] = apply(zx, q + 1, q, start)[1]
-
+    for q in (*range(OV), *range(own + OV, wide)):
+        wrap(zx, q + 1)
+    for q in (*range(OV), *range(own + OV, wide)):
+        for start in range(0, ny, ROWS):
+            vx[q, pl.ds(start, ROWS), :] = apply(zx, q + 1, q, start)[1]
     sent(SPILL0)
-    precondition(vx, 2, SPILL1, 1, z1x, 1)
+    precondition(vx, 2, SPILL1)
 
     sums = lax.fori_loop(0, n, lambda i, s: s + cast[2, i], jnp.zeros((1, nz), F32))
     rz = total_of(jnp.where(lane == nz - 2, sums, 0.0))
     za = total_of(jnp.where(lane == nz - 1, sums, 0.0))
     step0 = rz / za
 
-    @pl.loop(0, own)
-    def _(p):
-        z1x[p + 1, body, :] = zx[OV + 1 + p, body, :] - step0 * z1x[p + 1, body, :]
-
-    send(NEAR1)
-    received(NEAR1)
-
-    @pl.loop(0, own + 2)
-    def _(p):
-        wrap(z1x, p)
+    def second_direction(plane):
+        gather_part(1, z1x, 1, plane)
+        z1x[plane + 1, body, :] = (
+            zx[OV + 1 + plane, body, :] - step0 * z1x[plane + 1, body, :]
+        )
 
     def second_image(p, sums):
         rz1, za1, zv = sums
@@ -481,7 +474,20 @@
             zv += fold(centre * before)
         return rz1, za1, zv
 
-    rz1, za1, zv = lax.fori_loop(0, own, second_image, (zero, zero, zero))
+    for plane in ends:
+        second_direction(plane)
+    send(NEAR1)
+    for plane in middle:
+        second_direction(plane)
+    for plane in range(own):
+        wrap(z1x, plane + 1)
+    sums = (zero, zero, zero)
+    for plane in middle:
+        sums = second_image(plane, sums)
+    received(NEAR1)
+    for plane in ends:
+        sums = second_image(plane, sums)
+    rz1, za1, zv = sums
     row = jnp.where(lane == 0, total_of(rz1), 0.0)
     row = jnp.where(lane == 1, total_of(za1), row)
     row = jnp.where(lane == 2, total_of(zv), row)
@@ -534,7 +540,8 @@
             pltpu.VMEM((wide, ny, nz), F32),
             pltpu.VMEM((wide, ny, nz), F32),
             pltpu.VMEM((wide, ny, nz), F32),
-            pltpu.VMEM((2, wide + 2, tall, nz), F32),
+            pltpu.VMEM((wide + 2, tall, nz), F32),
+            pltpu.VMEM((wide + 2, tall, nz), F32),
             pltpu.VMEM((2, 2, OV, ny, nz), F32),
             pltpu.VMEM((wide + 2, tall, nz), F32),
             pltpu.VMEM((own + 2, tall, nz), F32),
@@ -558,7 +565,7 @@
             dma((6,)),
         ],
         compiler_params=pltpu.CompilerParams(
-            collective_id=0, has_side_effects=True, vmem_limit_bytes=48 * 1024 * 1024
+            collective_id=0, has_side_effects=True, vmem_limit_bytes=63 * 1024 * 1024
         ),
         name="schwarz_cg",
     )(pressure_source, permeability, widths, extents, coarse_owner, coarse_inverse, basis)

time: 65 us -> 52 us (0.80)
  Pallas kernels: 58 us -> 46.5 us
  local copies, waits for them, and re-layouts: 4.85 us -> 3.34 us
    pallas_call x1, Pallas kernels: 58 us -> 46.5 us  [per_device(): pl.pallas_call(functools.partial(kernel, n), out_shape=(out, out), in_spe...]
    unnamed x10 -> x2, local copies, waits for them, and re-layouts: 4.85 us -> 3.34 us
where the time goes in v3:
time: 52 us; the launch traced here: 51.8 us
  Pallas kernels  46.5 us (89%)
  local copies, waits for them, and re-layouts  3.34 us (6%)
  between operations  1.93 us (4%)
    pallas_call x1, Pallas kernels, per_device(): pl.pallas_call(functools.partial(kernel, n), out_shape=(out, out), in_spe...  46.5 us
    unnamed x2, local copies, waits for them, and re-layouts  3.34 us

profile of v3, /device:TPU:0, one launch (start us, length us, event | category | flops | bytes accessed | tf_op | source)
XLA Modules:
  0.0 51.8 jit_solution(7397344718443164756)
XLA Ops:
  1.9 46.5 %schwarz_cg.1 = (f32[4,128,128]{2,1,0:T(8,128)}, f32[4,128,128]{2,1,0:T(8,128)}) custom-call(f32[4,128,128]{2,1,0:T(8,128)} %src_hbm.1, f32[4,128,128]{2,1,0:T(8,128)} %perm_hbm.1, s32[1]{0:T(128)S(6)} %copy.11.width_hbm, s32[1]{0:T(128)S(6)} %copy.12.extent_hbm, s32[16]{0:T(128)} %owner_hbm.1, f32[40,640]{1,0:T(8,128)} %inverse_hbm.1, ...), custom_call_target="tpu_custom_call" | custom-call | tf_op jit(solution)/shard_map/schwarz_cg/pallas_call | solution.py:529
  48.4 1.7 %copy.13 = f32[4,128,128]{2,1,0:T(8,128)} copy(f32[4,128,128]{2,1,0:T(8,128)} %get-tuple-element.4) | data formatting | bytes 524288
  50.1 1.7 %copy.14 = f32[4,128,128]{2,1,0:T(8,128)} copy(f32[4,128,128]{2,1,0:T(8,128)} %get-tuple-element.5) | data formatting | bytes 524288

commit v4 on v3

--- a/solution.py
+++ b/solution.py
@@ -393,21 +393,21 @@
 
     zero = jnp.zeros((8, nz), F32)
 
+    for p in range(OV + 1, own + OV + 1):
+        order_couplings(p)
+    for p in range(OV + 1, own + OV - 1):
+        couple(p)
+    for p in range(OV, own + OV):
+        reorder(fx, p, fp, p, 0)
     broadcast(0, project(fx, OV, True))
     received(PERM)
 
-    @pl.loop(0, wide + 2)
-    def _(p):
+    for p in (*range(OV + 1), *range(own + OV + 1, wide + 2)):
         order_couplings(p)
-
-    @pl.loop(0, wide)
-    def _(p):
+    for p in (*range(OV + 1), *range(own + OV - 1, wide)):
         couple(p)
-
     received(RHS)
-
-    @pl.loop(0, wide)
-    def _(p):
+    for p in (*range(OV), *range(own + OV, wide)):
         reorder(fx, p, fp, p, 0)
 
     precondition(fp, 0, SPILL0)

time: 52 us -> 51.5 us (level)
  no operation moved by 1% of the time
where the time goes in v4:
time: 51.5 us; the launch traced here: 51.3 us
  Pallas kernels  46 us (89%)
  local copies, waits for them, and re-layouts  3.34 us (6%)
  between operations  1.93 us (4%)
    pallas_call x1, Pallas kernels, per_device(): pl.pallas_call(functools.partial(kernel, n), out_shape=(out, out), in_spe...  46 us
    unnamed x2, local copies, waits for them, and re-layouts  3.34 us

profile of v4, /device:TPU:0, one launch (start us, length us, event | category | flops | bytes accessed | tf_op | source)
XLA Modules:
  0.0 51.3 jit_solution(11777681360716161200)
XLA Ops:
  1.9 46.0 %schwarz_cg.1 = (f32[4,128,128]{2,1,0:T(8,128)}, f32[4,128,128]{2,1,0:T(8,128)}) custom-call(f32[4,128,128]{2,1,0:T(8,128)} %src_hbm.1, f32[4,128,128]{2,1,0:T(8,128)} %perm_hbm.1, s32[1]{0:T(128)S(6)} %copy.11.width_hbm, s32[1]{0:T(128)S(6)} %copy.12.extent_hbm, s32[16]{0:T(128)} %owner_hbm.1, f32[40,640]{1,0:T(8,128)} %inverse_hbm.1, ...), custom_call_target="tpu_custom_call" | custom-call | tf_op jit(solution)/shard_map/schwarz_cg/pallas_call | solution.py:529
  48.0 1.7 %copy.13 = f32[4,128,128]{2,1,0:T(8,128)} copy(f32[4,128,128]{2,1,0:T(8,128)} %get-tuple-element.4) | data formatting | bytes 524288
  49.6 1.7 %copy.14 = f32[4,128,128]{2,1,0:T(8,128)} copy(f32[4,128,128]{2,1,0:T(8,128)} %get-tuple-element.5) | data formatting | bytes 524288
